TPU v7x, 256 devices: a whole 4x4x8 slice. The times are simulated.
256 devices in a mesh: path: 64 (over y, z, core), dp: 4 (over x).
Axes of the slice: x: 4, y: 4, z: 8, core: 2. Of those that a mesh axis runs over, the one named last changes fastest.
Arguments:
- path_params: bfloat16 [128, 32, 8192], P('path', None, 'dp'), may hold values from -6 to 6
- path_module: int32 [128], replicated, may hold values from 0 to 15, as said below
- owner_of: int32 [16], replicated, may hold values from 0 to 63, as said below
- outer_params: float32 [64, 32, 8192], P('path', None, 'dp'), may hold values from -6 to 6
- momentum: float32 [64, 32, 8192], P('path', None, 'dp'), may hold values from -6 to 6
Outputs:
- new_outer: float32 [64, 32, 8192], P('path', None, 'dp')
- new_momentum: float32 [64, 32, 8192], P('path', None, 'dp')
- refreshed: bfloat16 [128, 32, 8192], P('path', None, 'dp')
Inputs may be any that keep to these rules, and one draw needn't show every extreme that they name: `path_module`: every module is used by at least one path; counts are uneven. `owner_of`: distinct owner slots, one for each module.
All inputs are finite; a program needn't handle non-finite values.
Results may differ from a plain program's by a relative error of at most 0.0004.
Values may be sent and summed in bfloat16 or wider, within the bound.
A program may use at most 64 MiB of HBM per device.

v0:
```python
import jax
import jax.numpy as jnp
from jax import lax
from jax.sharding import PartitionSpec as P

FF = 8192
R = 32


def local(path_params, path_module, owner_of, outer_params, momentum):
    high = lax.Precision.HIGHEST
    pdev = path_params.shape[0]
    slots = outer_params.shape[0]
    modules = owner_of.shape[0]
    group = lax.axis_index("path")
    module_ids = jnp.arange(modules, dtype=jnp.int32)
    mine = group * slots + jnp.arange(slots, dtype=jnp.int32)
    owned = (owner_of[None, :] == mine[:, None]).astype(jnp.float32)
    every_hot = (path_module[:, None] == module_ids[None, :]).astype(jnp.float32)
    counts = jnp.sum(every_hot, axis=0)
    owned_count = jnp.dot(owned, counts, precision=high)
    held = jnp.sum(owned, axis=1) > 0.5
    local_ids = lax.dynamic_slice_in_dim(path_module, group * pdev, pdev)
    local_owner = jnp.sum(
        jnp.where(local_ids[:, None] == module_ids[None, :], owner_of[None, :], 0), axis=1
    )
    hot = (path_module[:, None] == module_ids[None, :]).astype(jnp.float32)
    weights = jnp.dot(owned, hot.T, precision=high)
    sums = jnp.einsum(
        "sk,krc->src",
        weights,
        lax.all_gather(path_params, "path", axis=0, tiled=True).astype(jnp.float32),
        precision=high,
    )
    mean = sums / jnp.maximum(owned_count, 1.0)[:, None, None]
    pseudo = jnp.where(held[:, None, None], outer_params - mean, 0.0)
    squares = lax.psum(jnp.sum(pseudo * pseudo, axis=(1, 2)), "dp")
    limit = 0.5 * jnp.sqrt(jnp.float32(R * FF))
    factor = jnp.minimum(1.0, limit / jnp.sqrt(squares + 1e-06))
    grad = factor[:, None, None] * pseudo
    velocity = 0.9 * momentum + grad
    theta = outer_params - 0.7 * (0.9 * velocity + grad)
    new_outer = jnp.where(held[:, None, None], theta, outer_params)
    new_momentum = jnp.where(held[:, None, None], velocity, momentum)
    slab_half = new_outer.astype(jnp.bfloat16)
    everyone = lax.all_gather(slab_half, "path", axis=0, tiled=True)
    targets = jnp.arange(everyone.shape[0], dtype=jnp.int32)
    select = (local_owner[:, None] == targets[None, :]).astype(jnp.bfloat16)
    refreshed = jnp.einsum("po,orc->prc", select, everyone, preferred_element_type=jnp.float32)
    return (new_outer, new_momentum, refreshed.astype(jnp.bfloat16))


def solution(mesh):
    return jax.shard_map(
        local,
        mesh=mesh,
        in_specs=(P("path", None, "dp"), P(), P(), P("path", None, "dp"), P("path", None, "dp")),
        out_specs=(P("path", None, "dp"), P("path", None, "dp"), P("path", None, "dp")),
        check_vma=False,
    )
```

profile of v0, /device:TPU:1, one launch (start us, length us, event | category | flops | bytes accessed | tf_op | source)
XLA Modules:
  0.0 257.1 jit_solution(845183229586867996)
XLA Ops:
  7.2 0.0 copy-start.3
  7.2 0.0 copy-start.2
  7.2 0.0 copy-start
  7.2 0.0 copy-start.1
  7.2 0.0 all-gather.3.cloned.1.call-start
  7.3 0.7 all-gather.3.cloned.1.call-update
  7.9 0.0 all-gather.5.cloned.1.call-start
  8.0 0.8 convert_reduce_fusion
  8.8 1.3 convert_reduce_fusion.1
  11.3 0.8 convolution_bitcast_fusion
  12.1 102.9 %all-gather.3.cloned.1.call-done = bf16[128,32,2048]{2,1,0:T(8,128)(2,1)} async-done(((bf16[2,32,2048]{2,1,0:T(8,128)(2,1)}), bf16[128,32,2048]{2,1,0:T(8,128)(2,1)}) %all-gather.3.cloned.1.call-update) | async-done | bytes 16777232 | tf_op jit(solution)/shard_map/all_gather | solution.py:32
  115.0 30.4 %fusion = f32[1,32,2048]{2,0,1:T(1,128)S(1)} fusion(f32[128,1,1]{0,1,2:T(1,128)S(1)} %convolution_bitcast_fusion, bf16[128,32,2048]{2,1,0:T(8,128)(2,1)} %all-gather.3.cloned.1.call-done), kind=kOutput, calls=%fused_computation | convolution fusion | flops 100663296 | bytes 17039872 | tf_op jit(solution)/shard_map/sk,krc->src/dot_general | solution.py:29
  145.4 0.0 copy-done
  145.4 0.7 multiply_reduce_fusion
  146.1 9.2 %psum.7 = f32[1]{0:T(128)} all-reduce(f32[1]{0:T(128)} %bitcast.5), channel_id=1, replica_groups=mesh['path'=64,'dp'=4] {'dp'}, use_global_device_ids=true, to_apply=%region_3.4 | all-reduce | flops 1 | bytes 8 | tf_op jit(solution)/shard_map/psum | solution.py:37
  156.0 0.0 copy-done.1
  156.0 1.0 fusion.16
  157.0 0.0 all-gather.5.cloned.1.call-update
  157.1 0.0 copy-done.3
  157.1 0.1 dynamic_slice.3
  157.1 0.0 copy-done.2
  157.1 0.2 fusion.13
  157.3 79.8 %all-gather.5.cloned.1.call-done = bf16[64,32,2048]{2,1,0:T(8,128)(2,1)} async-done(((bf16[1,32,2048]{2,1,0:T(8,128)(2,1)}), bf16[64,32,2048]{2,1,0:T(8,128)(2,1)}) %all-gather.5.cloned.1.call-update) | async-done | bytes 8388624 | tf_op jit(solution)/shard_map/all_gather | solution.py:46
  237.2 12.3 %fusion.4 = bf16[2,32,2048]{2,0,1:T(2,128)(2,1)S(1)} fusion(bf16[64,32,2048]{2,1,0:T(8,128)(2,1)} %all-gather.5.cloned.1.call-done, s32[2]{0:T(128)S(1)} %fusion.13), kind=kOutput, calls=%fused_computation.4 | convolution fusion | flops 16908416 | bytes 8650760 | tf_op jit(solution)/shard_map/po,orc->prc/dot_general | solution.py:49
  249.5 0.8 copy.20
Async XLA Ops:
  7.2 149.9 %copy-start.3 = (s32[128]{0:T(128)S(1)}, s32[128]{0:T(128)}, u32[]{:S(2)}) copy-start(s32[128]{0:T(128)} %param.6) | copy-start | bytes 1540
  7.2 150.0 %copy-start.2 = (s32[16]{0:T(128)S(1)}, s32[16]{0:T(128)}, u32[]{:S(2)}) copy-start(s32[16]{0:T(128)} %param.7) | copy-start | bytes 196
  7.2 138.2 %copy-start = (f32[1,32,2048]{2,1,0:T(8,128)S(1)}, f32[1,32,2048]{2,1,0:T(8,128)}, u32[]{:S(2)}) copy-start(f32[1,32,2048]{2,1,0:T(8,128)} %param.8) | copy-start | bytes 786436
  7.2 148.8 %copy-start.1 = (f32[1,32,2048]{2,1,0:T(8,128)S(1)}, f32[1,32,2048]{2,1,0:T(8,128)}, u32[]{:S(2)}) copy-start(f32[1,32,2048]{2,1,0:T(8,128)} %param.9) | copy-start | bytes 786436
  7.2 107.8 %all-gather.3.cloned.1.call-start = ((), (), s32[]{:S(2)}) async-start(), calls=%async_computation | async-start | bytes 17039360 | tf_op jit(solution)/shard_map/all_gather | solution.py:32
  7.9 229.2 %all-gather.5.cloned.1.call-start = ((), (), s32[]{:S(2)}) async-start(), calls=%async_computation.1 | async-start | bytes 8519680 | tf_op jit(solution)/shard_map/all_gather | solution.py:46
Sparse Core Ops, SparseCore 0:
  10.8 104.1 all-gather.2
  157.2 79.9 all-gather.4
where the time goes:
time: 257 us
  waiting for transfers between devices  183 us (71%)
  matrix products  43.5 us (17%)
  between operations  16.1 us (6%)
  blocking collectives  9.19 us (4%)
  other arithmetic  3.93 us (2%)
    all_gather x1, waiting for transfers between devices, local(): lax.all_gather(path_params, 'path', axis=0, tiled=True).astype(jnp.float32)  103 us
    all_gather x1, waiting for transfers between devices, local(): everyone = lax.all_gather(slab_half, 'path', axis=0, tiled=True)  79.8 us
    dot_general x1, matrix products, local(): jnp.einsum('sk,krc->src', weights, lax.all_gather(path_params, 'path', ax...  30.4 us
    dot_general x1, matrix products, local(): jnp.einsum('po,orc->prc', select, everyone, preferred_element_type=jnp.fl...  12.3 us
    psum x1, blocking collectives, local(): squares = lax.psum(jnp.sum(pseudo * pseudo, axis=(1, 2)), 'dp')  9.19 us
  transfers between devices with their start and end apart: 2, of which 2 were waited for; matrix products, arithmetic and copies ran while one was open for 1% of the time, Pallas kernels for 0%

commit v1 on v0

v1 whole, which is shorter than its diff:
```python
import jax
import jax.numpy as jnp
from jax import lax
from jax.sharding import PartitionSpec as P

FF = 8192
R = 32


def to_chunks(slab):
    n = slab.shape[0]
    return slab.reshape(n, 4, 8, 16, 128).transpose(1, 3, 0, 2, 4).reshape(64, n, 8, 128)


def from_chunks(chunks):
    n = chunks.shape[1]
    return chunks.reshape(4, 16, n, 8, 128).transpose(2, 0, 3, 1, 4).reshape(n, 32, 2048)


def exchange(chunks):
    return lax.all_to_all(chunks, "path", 0, 0, tiled=True)


def local(path_params, path_module, owner_of, outer_params, momentum):
    modules = owner_of.shape[0]
    group = lax.axis_index("path")
    module_ids = jnp.arange(modules, dtype=jnp.int32)
    slot_ids = jnp.arange(64, dtype=jnp.int32)
    slot_of_path = jnp.sum(
        jnp.where(path_module[:, None] == module_ids[None, :], owner_of[None, :], 0), axis=1
    )
    held = jnp.any(owner_of == group)
    hot = slot_of_path[None, :] == slot_ids[:, None]
    counts = jnp.sum(hot.astype(jnp.float32), axis=1)

    mine = exchange(to_chunks(path_params)).reshape(128, 1024)
    sums = jnp.dot(hot.astype(jnp.bfloat16), mine, preferred_element_type=jnp.float32)
    mean = sums / jnp.maximum(counts, 1.0)[:, None]
    mean = from_chunks(exchange(mean.reshape(64, 1, 8, 128)))

    pseudo = jnp.where(held, outer_params - mean, 0.0)
    squares = lax.psum(jnp.sum(pseudo * pseudo), "dp")
    limit = 0.5 * jnp.sqrt(jnp.float32(R * FF))
    factor = jnp.minimum(1.0, limit / jnp.sqrt(squares + 1e-06))
    grad = factor * pseudo
    velocity = 0.9 * momentum + grad
    theta = outer_params - 0.7 * (0.9 * velocity + grad)
    new_outer = jnp.where(held, theta, outer_params)
    new_momentum = jnp.where(held, velocity, momentum)

    slabs = exchange(to_chunks(new_outer.astype(jnp.bfloat16))).reshape(64, 1024)
    chosen = jnp.dot(hot.astype(jnp.bfloat16).T, slabs, preferred_element_type=jnp.float32)
    refreshed = from_chunks(exchange(chosen.astype(jnp.bfloat16).reshape(64, 2, 8, 128)))
    return (new_outer, new_momentum, refreshed)


def solution(mesh):
    return jax.shard_map(
        local,
        mesh=mesh,
        in_specs=(P("path", None, "dp"), P(), P(), P("path", None, "dp"), P("path", None, "dp")),
        out_specs=(P("path", None, "dp"), P("path", None, "dp"), P("path", None, "dp")),
        check_vma=False,
    )
```

time: 257 us -> 95.8 us (0.37)
  waiting for transfers between devices: 183 us -> 23.1 us
  matrix products: 43.5 us -> 0.44 us
  blocking collectives: 9.19 us -> 43.9 us
  starting transfers between devices: 0.08 us -> 19.4 us
  between operations: 16.1 us -> 1.41 us
    all_gather x2 -> x0, waiting for transfers between devices: 183 us -> none  [the longest x1 103 us: local(): lax.all_gather(path_params, 'path', axis=0, tiled=True).astype(jnp.float32)]
    dot_general x3 -> x2, matrix products: 43.5 us -> 0.44 us  [the longest x1 0.27 us: local(): jnp.dot(hot.astype(jnp.bfloat16).T, slabs, preferred_element_type=jnp.flo...]
    all_to_all x0 -> x2, blocking collectives: none -> 34.9 us  [exchange(): return lax.all_to_all(chunks, 'path', 0, 0, tiled=True)]
    all_to_all x0 -> x2, waiting for transfers between devices: none -> 23.1 us  [exchange(): return lax.all_to_all(chunks, 'path', 0, 0, tiled=True)]
    all_to_all x0 -> x2, starting transfers between devices: none -> 19.4 us  [exchange(): return lax.all_to_all(chunks, 'path', 0, 0, tiled=True)]
where the time goes in v1:
time: 95.8 us; the launch traced here: 95.4 us
  blocking collectives  43.9 us (46%)
  waiting for transfers between devices  23.1 us (24%)
  starting transfers between devices  19.4 us (20%)
  other arithmetic  3.89 us (4%)
  local copies, waits for them, and re-layouts  3.26 us (3%)
  between operations  1.41 us (1%)
    all_to_all x2, blocking collectives, exchange(): return lax.all_to_all(chunks, 'path', 0, 0, tiled=True)  34.9 us
    all_to_all x2, waiting for transfers between devices, exchange(): return lax.all_to_all(chunks, 'path', 0, 0, tiled=True)  23.1 us
    all_to_all x2, starting transfers between devices, exchange(): return lax.all_to_all(chunks, 'path', 0, 0, tiled=True)  19.4 us
    psum x1, blocking collectives, local(): squares = lax.psum(jnp.sum(pseudo * pseudo), 'dp')  9.07 us
  transfers between devices with their start and end apart: 2, of which 2 were waited for; matrix products, arithmetic and copies ran while one was open for 1% of the time, Pallas kernels for 0%

profile of v1, /device:TPU:1, one launch (start us, length us, event | category | flops | bytes accessed | tf_op | source)
XLA Modules:
  0.0 95.4 jit_solution(3166064015408587307)
XLA Ops:
  0.6 1.7 %copy.14 = bf16[4,16,2,8,128]{4,3,2,1,0:T(8,128)(2,1)} copy(bf16[4,16,2,8,128]{4,3,1,0,2:T(8,128)(2,1)} %bitcast.47) | data formatting | bytes 524288 | tf_op jit(solution)/shard_map/transpose | solution.py:12
  2.3 0.0 copy-start.2
  2.3 0.0 copy-start.3
  2.3 13.3 %all-to-all-start = ((bf16[64,2,8,128]{3,2,1,0:T(8,128)(2,1)}), bf16[64,2,8,128]{3,2,1,0:T(8,128)(2,1)S(1)}, u32[]{:S(2)}, u32[]{:S(2)}) async-start(bf16[64,2,8,128]{3,2,1,0:T(8,128)(2,1)} %bitcast.2), calls=%async_computation | async-start | bytes 524288 | tf_op jit(solution)/shard_map/all_to_all | solution.py:21
  15.6 0.0 copy-done.2
  15.6 0.0 copy-done.3
  15.6 0.1 select_reduce_fusion
  15.7 0.1 convert_reduce_fusion
  15.9 11.8 %all-to-all-done = bf16[64,2,8,128]{3,2,1,0:T(8,128)(2,1)S(1)} async-done(((bf16[64,2,8,128]{3,2,1,0:T(8,128)(2,1)}), bf16[64,2,8,128]{3,2,1,0:T(8,128)(2,1)S(1)}, u32[]{:S(2)}, u32[]{:S(2)}) %all-to-all-start) | async-done | bytes 262176 | tf_op jit(solution)/shard_map/all_to_all | solution.py:21
  27.6 0.2 fusion
  27.8 0.8 copy.18
  28.6 0.0 copy-start
  28.6 6.2 %all-to-all-start.1 = ((f32[64,1,8,128]{3,2,1,0:T(8,128)}), f32[64,1,8,128]{3,2,1,0:T(8,128)S(1)}, u32[]{:S(2)}, u32[]{:S(2)}) async-start(f32[64,1,8,128]{3,2,1,0:T(8,128)} %bitcast.3), calls=%async_computation.1 | async-start | bytes 524288 | tf_op jit(solution)/shard_map/all_to_all | solution.py:21
  34.7 0.7 compare_reduce_fusion
  35.5 11.3 %all-to-all-done.1 = f32[64,1,8,128]{3,2,1,0:T(8,128)S(1)} async-done(((f32[64,1,8,128]{3,2,1,0:T(8,128)}), f32[64,1,8,128]{3,2,1,0:T(8,128)S(1)}, u32[]{:S(2)}, u32[]{:S(2)}) %all-to-all-start.1) | async-done | bytes 262176 | tf_op jit(solution)/shard_map/all_to_all | solution.py:21
  46.7 0.0 copy-done
  46.7 0.0 copy-start.1
  46.7 1.4 %multiply_reduce_fusion = f32[]{:T(128)} fusion(f32[1,32,2048]{2,1,0:T(8,128)S(1)} %copy-done, f32[1,32,2048]{2,1,0:T(8,128)S(1)} %bitcast.41, pred[]{:T(512)} %compare_reduce_fusion), kind=kLoop, calls=%fused_computation.8 | loop fusion | flops 262143 | bytes 524293 | tf_op jit(solution)/shard_map/reduce_sum | solution.py:42
  48.1 9.1 %psum.7 = f32[]{:T(128)} all-reduce(f32[]{:T(128)} %multiply_reduce_fusion), channel_id=1, replica_groups=mesh['path'=64,'dp'=4] {'dp'}, use_global_device_ids=true, to_apply=%region_4.5 | all-reduce | flops 1 | bytes 8 | tf_op jit(solution)/shard_map/psum | solution.py:42
  57.9 0.0 copy-done.1
  57.9 1.6 %fusion.9 = (bf16[1,32,2048]{2,1,0:T(8,128)(2,1)S(1)}, f32[1,32,2048]{2,1,0:T(8,128)}, f32[1,32,2048]{2,1,0:T(8,128)}) fusion(f32[1,32,2048]{2,1,0:T(8,128)S(1)} %copy-done, f32[1,32,2048]{2,1,0:T(8,128)S(1)} %bitcast.42, f32[]{:T(128)S(6)} %min.3, f32[1,32,2048]{2,1,0:T(8,128)S(1)} %copy-done.1, pred[]{:T(512)} %compare_reduce_fusion), kind=kLoop, calls=%fused_computation.22 | loop fusion | flops 786432 | bytes 1441797 | tf_op jit(solution)/shard_map/convert_element_type | solution.py:51
  59.5 18.2 %all_to_all.20 = bf16[64,1,8,128]{3,2,1,0:T(8,128)(2,1)S(1)} all-to-all(bf16[64,1,8,128]{3,2,1,0:T(8,128)(2,1)S(1)} %bitcast.45), channel_id=1, replica_groups=mesh['path'=64,'dp'=4] {'path'}, dimensions={0} | all-to-all | bytes 262144 | tf_op jit(solution)/shard_map/all_to_all | solution.py:21
  77.7 0.3 fusion.1
  78.0 16.7 %all_to_all.21 = bf16[64,2,8,128]{3,2,1,0:T(8,128)(2,1)S(1)} all-to-all(bf16[64,2,8,128]{3,2,1,0:T(8,128)(2,1)S(1)} %bitcast.43), channel_id=1, replica_groups=mesh['path'=64,'dp'=4] {'path'}, dimensions={0} | all-to-all | bytes 524288 | tf_op jit(solution)/shard_map/all_to_all | solution.py:21
  94.7 0.8 copy.30
  (2 shorter events, 0.0 us)
Async XLA Ops:
  2.3 13.3 %copy-start.2 = (s32[128]{0:T(128)S(1)}, s32[128]{0:T(128)}, u32[]{:S(2)}) copy-start(s32[128]{0:T(128)} %param.6) | copy-start | bytes 1540
  2.3 13.3 %copy-start.3 = (s32[16]{0:T(128)S(1)}, s32[16]{0:T(128)}, u32[]{:S(2)}) copy-start(s32[16]{0:T(128)} %param.7) | copy-start | bytes 196
  2.3 25.3 %all-to-all-start = ((bf16[64,2,8,128]{3,2,1,0:T(8,128)(2,1)}), bf16[64,2,8,128]{3,2,1,0:T(8,128)(2,1)S(1)}, u32[]{:S(2)}, u32[]{:S(2)}) async-start(bf16[64,2,8,128]{3,2,1,0:T(8,128)(2,1)} %bitcast.2), calls=%async_computation | async-start | bytes 524288 | tf_op jit(solution)/shard_map/all_to_all | solution.py:21
  28.6 18.2 %copy-start = (f32[1,32,2048]{2,1,0:T(8,128)S(1)}, f32[1,32,2048]{2,1,0:T(8,128)}, u32[]{:S(2)}) copy-start(f32[1,32,2048]{2,1,0:T(8,128)} %param.8) | copy-start | bytes 786436
  28.6 18.2 %all-to-all-start.1 = ((f32[64,1,8,128]{3,2,1,0:T(8,128)}), f32[64,1,8,128]{3,2,1,0:T(8,128)S(1)}, u32[]{:S(2)}, u32[]{:S(2)}) async-start(f32[64,1,8,128]{3,2,1,0:T(8,128)} %bitcast.3), calls=%async_computation.1 | async-start | bytes 524288 | tf_op jit(solution)/shard_map/all_to_all | solution.py:21
  46.7 11.2 %copy-start.1 = (f32[1,32,2048]{2,1,0:T(8,128)S(1)}, f32[1,32,2048]{2,1,0:T(8,128)}, u32[]{:S(2)}) copy-start(f32[1,32,2048]{2,1,0:T(8,128)} %param.9) | copy-start | bytes 786436

commit v2 on v1

v2 whole, which is shorter than its diff:
```python
import jax
import jax.numpy as jnp
from jax import lax
from jax.experimental import pallas as pl
from jax.experimental.pallas import tpu as pltpu
from jax.sharding import PartitionSpec as P

FF = 8192
R = 32
MODULES = 16
N = 64
DP = 4
MESH = pl.DeviceIdType.MESH
F32 = jnp.float32
BF16 = jnp.bfloat16


def zig(j, middle):
    return middle + (1 - 2 * lax.rem(j, 2)) * lax.div(j + 1, 2)


def peer(me, k):
    y, z, core = lax.div(me, 16), lax.rem(lax.div(me, 2), 8), lax.rem(me, 2)
    dy = zig(lax.div(k, 16), 2)
    dz = zig(lax.rem(lax.div(k, 2), 8), 4)
    dc = 1 - lax.rem(k, 2)
    return lax.rem(y + dy, 4) * 16 + lax.rem(z + dz, 8) * 2 + lax.rem(core + dc, 2)


def rows(index, count):
    return pl.ds(pl.multiple_of(index * count, count), count)


def tile(index):
    return (rows(lax.div(index, 16), 8), rows(lax.rem(index, 16), 128))


def kernel(
    module_ref, owner_ref, x_hbm, outer_hbm, mom_hbm,
    new_outer_ref, new_mom_ref, fresh_ref,
    x_v, outer_v, mom_v, x_send, x_recv, outer_recv, mom_recv, mean_send, mean_slab,
    fresh_send, fresh_recv, dp_recv, vec_recv, weights, select,
    load_sem, send_sem, recv_sem,
):
    me = lax.axis_index("path")
    plane = lax.axis_index("dp")

    loads = [
        pltpu.make_async_copy(src.at[...], dst.at[...], load_sem.at[i])
        for i, (src, dst) in enumerate(((x_hbm, x_v), (outer_hbm, outer_v), (mom_hbm, mom_v)))
    ]
    for load in loads:
        load.start()

    barrier = pltpu.get_barrier_semaphore()

    @pl.loop(0, N - 1)
    def _(k):
        pl.semaphore_signal(barrier, inc=1, device_id={"path": peer(me, k)}, device_id_type=MESH)

    for k in range(1, DP):
        pl.semaphore_signal(
            barrier, inc=1, device_id={"dp": lax.rem(plane + k, DP)}, device_id_type=MESH
        )

    loads[0].wait()
    for half in range(2):
        first = x_v[0, 16 * half : 16 * half + 16, :].astype(F32)
        second = x_v[1, 16 * half : 16 * half + 16, :].astype(F32)
        for part in range(2):
            both = jnp.concatenate(
                [first[8 * part : 8 * part + 8], second[8 * part : 8 * part + 8]], axis=0
            ).astype(BF16)
            for column in range(16):
                chunk = (2 * half + part) * 16 + column
                x_send[16 * chunk : 16 * chunk + 16, :] = both[:, 128 * column : 128 * column + 128]
    loads[1].wait()
    loads[2].wait()

    pl.semaphore_wait(barrier, N - 1 + DP - 1)

    def send_all(stage, source, target):
        @pl.loop(0, N - 1)
        def _(k):
            to = peer(me, k)
            pltpu.make_async_remote_copy(
                src_ref=source(to), dst_ref=target, send_sem=send_sem.at[stage],
                recv_sem=recv_sem.at[stage], device_id={"path": to}, device_id_type=MESH,
            ).start()

    def wait(sem, ref, count):
        view = ref.at[pl.ds(0, count)]
        pltpu.make_async_copy(view, view, sem).wait()

    send_all(0, lambda to: x_send.at[rows(to, 16)], x_recv.at[rows(me, 16)])
    send_all(1, lambda to: outer_v.at[0].at[tile(to)], outer_recv.at[rows(me, 8)])
    send_all(2, lambda to: mom_v.at[0].at[tile(to)], mom_recv.at[rows(me, 8)])
    x_recv[rows(me, 16), :] = x_send[rows(me, 16), :]
    outer_recv[rows(me, 8), :] = outer_v[0, tile(me)[0], tile(me)[1]]
    mom_recv[rows(me, 8), :] = mom_v[0, tile(me)[0], tile(me)[1]]

    path_modules = jnp.broadcast_to(module_ref[...], (8, 128))
    slot_of_path = jnp.zeros((8, 128), jnp.int32)
    held_here = jnp.int32(0)
    for m in range(MODULES):
        owner = owner_ref[m]
        slot_of_path = jnp.where(path_modules == m, owner, slot_of_path)
        held_here = jnp.where(owner == me, 1, held_here)
    slot_of_path = slot_of_path.astype(F32)

    def iota(shape, axis):
        return lax.broadcasted_iota(jnp.int32, shape, axis)

    spread = (iota((128, 1024), 1) // 8 == iota((128, 1024), 0)).astype(F32).astype(BF16)
    across = jnp.dot(slot_of_path.astype(BF16), spread, preferred_element_type=F32)[0:1]
    shape = (N * 8, 1024)
    slot, row = (iota((N * 8, 1), 0) // 8).astype(F32), iota((N * 8, 1), 0) % 8
    hot = jnp.where((across == slot) & (iota((1, 1024), 1) % 8 == row), F32(1), F32(0))
    counts = jnp.sum(hot, axis=1, keepdims=True)
    weights[...] = hot.astype(BF16)
    down = jnp.sum(
        jnp.where(iota((1024, 128), 0) // 8 == iota((1024, 128), 1), slot_of_path[0:1], 0.0),
        axis=1, keepdims=True,
    )
    slot, row = (iota((1, N * 8), 1) // 8).astype(F32), iota((1, N * 8), 1) % 8
    select[...] = jnp.where(
        (down == slot) & (iota((1024, 1), 0) % 8 == row), F32(1), F32(0)
    ).astype(BF16)
    diagonal = iota((N * 8, 128), 0) // 8 == iota((N * 8, 128), 1)
    held = counts > 0.5
    divisor = jnp.maximum(counts, 1.0)

    wait(recv_sem.at[0], x_recv, 16 * (N - 1))
    sums = jnp.dot(weights[...], x_recv[...], preferred_element_type=F32)
    mean = sums / divisor
    mean_send[...] = mean
    wait(recv_sem.at[1], outer_recv, 8 * (N - 1))
    pseudo = jnp.where(held, outer_recv[...] - mean, 0.0)
    squares = jnp.sum(pseudo * pseudo, axis=1, keepdims=True)
    squares = jnp.sum(jnp.where(diagonal, squares, 0.0), axis=0, keepdims=True)

    dp_recv[pl.ds(plane, 1), :] = squares
    for k in range(1, DP):
        pltpu.make_async_remote_copy(
            src_ref=dp_recv.at[pl.ds(plane, 1)], dst_ref=dp_recv.at[pl.ds(plane, 1)],
            send_sem=send_sem.at[3], recv_sem=recv_sem.at[3],
            device_id={"dp": lax.rem(plane + k, DP)}, device_id_type=MESH,
        ).start()
    send_all(4, lambda to: mean_send.at[rows(to, 8)], mean_slab.at[tile(me)])
    mean_slab[tile(me)[0], tile(me)[1]] = mean_send[rows(me, 8), :]
    wait(recv_sem.at[3], dp_recv, DP - 1)
    everywhere = dp_recv[0:1] + dp_recv[1:2] + dp_recv[2:3] + dp_recv[3:4]

    vec_recv[pl.ds(me, 1), :] = everywhere
    send_all(5, lambda to: vec_recv.at[pl.ds(me, 1)], vec_recv.at[pl.ds(me, 1)])
    wait(recv_sem.at[2], mom_recv, 8 * (N - 1))
    limit = 0.5 * (float(R * FF) ** 0.5)
    wait(recv_sem.at[5], vec_recv, N - 1)
    total = jnp.sum(vec_recv[...], axis=0, keepdims=True)
    factors = jnp.minimum(1.0, limit / jnp.sqrt(total + 1e-06))

    factor = jnp.sum(jnp.where(diagonal, factors, 0.0), axis=1, keepdims=True)
    grad = factor * pseudo
    velocity = 0.9 * mom_recv[...] + grad
    theta = outer_recv[...] - 0.7 * (0.9 * velocity + grad)
    fresh_send[...] = jnp.dot(
        select[...], theta.astype(BF16), preferred_element_type=F32
    ).astype(BF16)
    send_all(6, lambda to: fresh_send.at[rows(to, 16)], fresh_recv.at[rows(me, 16)])
    fresh_recv[rows(me, 16), :] = fresh_send[rows(me, 16), :]

    held_slot = held_here > 0
    own_factor = jnp.sum(
        jnp.where(iota((1, 128), 1) == me, factors, 0.0), axis=1, keepdims=True
    )
    wait(recv_sem.at[4], mean_send, 8 * (N - 1))
    outer, mom = outer_v[0], mom_v[0]
    grad = own_factor * (outer - mean_slab[...])
    velocity = 0.9 * mom + grad
    theta = outer - 0.7 * (0.9 * velocity + grad)
    new_outer_ref[0] = jnp.where(held_slot, theta, outer)
    new_mom_ref[0] = jnp.where(held_slot, velocity, mom)

    wait(recv_sem.at[6], fresh_recv, 16 * (N - 1))
    for half in range(2):
        for column in range(16):
            top = fresh_recv[16 * (32 * half + column) : 16 * (32 * half + column) + 16, :].astype(F32)
            low = 16 * (32 * half + 16 + column)
            bottom = fresh_recv[low : low + 16, :].astype(F32)
            for path in range(2):
                fresh_ref[path, 16 * half : 16 * half + 16, 128 * column : 128 * column + 128] = (
                    jnp.concatenate(
                        [top[8 * path : 8 * path + 8], bottom[8 * path : 8 * path + 8]], axis=0
                    ).astype(BF16)
                )

    wait(send_sem.at[0], x_send, 16 * (N - 1))
    wait(send_sem.at[1], outer_recv, 8 * (N - 1))
    wait(send_sem.at[2], mom_recv, 8 * (N - 1))
    wait(send_sem.at[3], dp_recv, DP - 1)
    wait(send_sem.at[4], mean_send, 8 * (N - 1))
    wait(send_sem.at[5], vec_recv, N - 1)
    wait(send_sem.at[6], fresh_send, 16 * (N - 1))


def local(path_params, path_module, owner_of, outer_params, momentum):
    vmem = pl.BlockSpec(memory_space=pltpu.VMEM)
    anywhere = pl.BlockSpec(memory_space=pl.ANY)
    return pl.pallas_call(
        kernel,
        out_shape=(
            jax.ShapeDtypeStruct((1, R, 2048), F32),
            jax.ShapeDtypeStruct((1, R, 2048), F32),
            jax.ShapeDtypeStruct((2, R, 2048), BF16),
        ),
        in_specs=[vmem, pl.BlockSpec(memory_space=pltpu.SMEM), anywhere, anywhere, anywhere],
        out_specs=(vmem, vmem, vmem),
        scratch_shapes=[
            pltpu.VMEM((2, R, 2048), BF16),
            pltpu.VMEM((1, R, 2048), F32),
            pltpu.VMEM((1, R, 2048), F32),
            pltpu.VMEM((16 * N, 128), BF16),
            pltpu.VMEM((16 * N, 128), BF16),
            pltpu.VMEM((8 * N, 128), F32),
            pltpu.VMEM((8 * N, 128), F32),
            pltpu.VMEM((8 * N, 128), F32),
            pltpu.VMEM((R, 2048), F32),
            pltpu.VMEM((16 * N, 128), BF16),
            pltpu.VMEM((16 * N, 128), BF16),
            pltpu.VMEM((DP, 128), F32),
            pltpu.VMEM((N, 128), F32),
            pltpu.VMEM((8 * N, 1024), BF16),
            pltpu.VMEM((1024, 8 * N), BF16),
            pltpu.SemaphoreType.DMA((3,)),
            pltpu.SemaphoreType.DMA((7,)),
            pltpu.SemaphoreType.DMA((7,)),
        ],
        compiler_params=pltpu.CompilerParams(
            collective_id=0, has_side_effects=True, vmem_limit_bytes=48 << 20
        ),
    )(path_module.reshape(1, 128), owner_of, path_params, outer_params, momentum)


def solution(mesh):
    return jax.shard_map(
        local,
        mesh=mesh,
        in_specs=(P("path", None, "dp"), P(), P(), P("path", None, "dp"), P("path", None, "dp")),
        out_specs=(P("path", None, "dp"), P("path", None, "dp"), P("path", None, "dp")),
        check_vma=False,
    )
```

time: 95.8 us -> 55.8 us (0.58)
  Pallas kernels: 0 us -> 49.4 us
  blocking collectives: 43.9 us -> 0 us
  waiting for transfers between devices: 23.1 us -> 0 us
  starting transfers between devices: 19.4 us -> 0 us
  other arithmetic: 3.89 us -> 0 us
  local copies, waits for them, and re-layouts: 3.26 us -> 5.61 us
    pallas_call x0 -> x1, Pallas kernels: none -> 49.4 us  [local(): pl.pallas_call(kernel, out_shape=(jax.ShapeDtypeStruct((1, R, 2048), F32)...]
    all_to_all x2 -> x0, blocking collectives: 34.9 us -> none  [exchange(): return lax.all_to_all(chunks, 'path', 0, 0, tiled=True)]
    all_to_all x2 -> x0, waiting for transfers between devices: 23.1 us -> none  [exchange(): return lax.all_to_all(chunks, 'path', 0, 0, tiled=True)]
    all_to_all x2 -> x0, starting transfers between devices: 19.4 us -> none  [exchange(): return lax.all_to_all(chunks, 'path', 0, 0, tiled=True)]
    psum x1 -> x0, blocking collectives: 9.07 us -> none  [local(): squares = lax.psum(jnp.sum(pseudo * pseudo), 'dp')]
    unnamed x10 -> x13, local copies, waits for them, and re-layouts: 0.81 us -> 5.61 us
    transpose x1 -> x0, local copies, waits for them, and re-layouts: 1.7 us -> none  [to_chunks(): slab.reshape(n, 4, 8, 16, 128).transpose(1, 3, 0, 2, 4)]
    reduce_sum x3 -> x0, other arithmetic: 1.6 us -> none  [the longest x1 1.4 us: local(): squares = lax.psum(jnp.sum(pseudo * pseudo), 'dp')]
  transfers between devices with their start and end apart: 2 -> 0, of which waited for: 2 -> 0; matrix products, arithmetic and copies ran while one was open for 1% -> 0% of each run, Pallas kernels for 0% -> 0%
where the time goes in v2:
time: 55.8 us; the launch traced here: 55.7 us
  Pallas kernels  49.4 us (89%)
  local copies, waits for them, and re-layouts  5.61 us (10%)
  between operations  0.66 us (1%)
    pallas_call x1, Pallas kernels, local(): pl.pallas_call(kernel, out_shape=(jax.ShapeDtypeStruct((1, R, 2048), F32)...  49.4 us
    unnamed x13, local copies, waits for them, and re-layouts  5.61 us

profile of v2, /device:TPU:1, one launch (start us, length us, event | category | flops | bytes accessed | tf_op | source)
XLA Modules:
  0.0 55.7 jit_solution(18406489969124661649)
XLA Ops:
  0.6 0.0 copy-start.4
  0.6 0.0 copy-start.3
  0.7 0.6 %copy-done.4 = s32[16]{0:T(128)S(1)} copy-done((s32[16]{0:T(128)S(1)}, s32[16]{0:T(128)}, u32[]{:S(2)}) %copy-start.4) | copy-done | bytes 88
  1.3 0.0 copy-done.3
  1.3 0.0 copy-start
  1.3 0.9 %copy-done = bf16[2,32,2048]{2,1,0:T(8,128)(2,1)S(1)} copy-done((bf16[2,32,2048]{2,1,0:T(8,128)(2,1)S(1)}, bf16[2,32,2048]{2,1,0:T(8,128)(2,1)}, u32[]{:S(2)}) %copy-start) | copy-done | bytes 262168
  2.3 0.0 copy-start.1
  2.3 0.9 %copy-done.1 = f32[1,32,2048]{2,1,0:T(8,128)S(1)} copy-done((f32[1,32,2048]{2,1,0:T(8,128)S(1)}, f32[1,32,2048]{2,1,0:T(8,128)}, u32[]{:S(2)}) %copy-start.1) | copy-done | bytes 262168
  3.2 0.0 copy-start.2
  3.2 0.9 %copy-done.2 = f32[1,32,2048]{2,1,0:T(8,128)S(1)} copy-done((f32[1,32,2048]{2,1,0:T(8,128)S(1)}, f32[1,32,2048]{2,1,0:T(8,128)}, u32[]{:S(2)}) %copy-start.2) | copy-done | bytes 262168
  4.2 49.4 %shard_map.76 = (f32[1,32,2048]{2,1,0:T(8,128)S(1)}, f32[1,32,2048]{2,1,0:T(8,128)S(1)}, bf16[2,32,2048]{2,1,0:T(8,128)(2,1)S(1)}) custom-call(s32[1,128]{1,0:T(1,128)S(1)} %bitcast.1, s32[16]{0:T(128)S(1)} %copy-done.4, bf16[2,32,2048]{2,1,0:T(8,128)(2,1)S(1)} %copy-done, f32[1,32,2048]{2,1,0:T(8,128)S(1)} %copy-done.1, f32[1,32,2048]{2,1,0:T(8,128)S(1)} %copy-done.2), custom_call_target="tpu_custom_call" | custom-call | tf_op jit(solution)/shard_map/pallas_call | solution.py:209
  53.5 0.7 %copy.11 = f32[1,32,2048]{2,1,0:T(8,128)} copy(f32[1,32,2048]{2,1,0:T(8,128)S(1)} %get-tuple-element.6) | data formatting | bytes 524288
  54.2 0.7 %copy.12 = f32[1,32,2048]{2,1,0:T(8,128)} copy(f32[1,32,2048]{2,1,0:T(8,128)S(1)} %get-tuple-element.7) | data formatting | bytes 524288
  55.0 0.7 %copy.13 = bf16[2,32,2048]{2,1,0:T(8,128)(2,1)} copy(bf16[2,32,2048]{2,1,0:T(8,128)(2,1)S(1)} %get-tuple-element.8) | data formatting | bytes 524288
Async XLA Ops:
  0.6 0.7 %copy-start.4 = (s32[16]{0:T(128)S(1)}, s32[16]{0:T(128)}, u32[]{:S(2)}) copy-start(s32[16]{0:T(128)} %owner_ref.1) | copy-start | bytes 196
  0.6 0.7 %copy-start.3 = (s32[128]{0:T(128)S(1)}, s32[128]{0:T(128)}, u32[]{:S(2)}) copy-start(s32[128]{0:T(128)} %param.6) | copy-start | bytes 1540
  1.3 0.9 %copy-start = (bf16[2,32,2048]{2,1,0:T(8,128)(2,1)S(1)}, bf16[2,32,2048]{2,1,0:T(8,128)(2,1)}, u32[]{:S(2)}) copy-start(bf16[2,32,2048]{2,1,0:T(8,128)(2,1)} %x_hbm.1) | copy-start | bytes 786436
  2.3 0.9 %copy-start.1 = (f32[1,32,2048]{2,1,0:T(8,128)S(1)}, f32[1,32,2048]{2,1,0:T(8,128)}, u32[]{:S(2)}) copy-start(f32[1,32,2048]{2,1,0:T(8,128)} %outer_hbm.1) | copy-start | bytes 786436
  3.2 0.9 %copy-start.2 = (f32[1,32,2048]{2,1,0:T(8,128)S(1)}, f32[1,32,2048]{2,1,0:T(8,128)}, u32[]{:S(2)}) copy-start(f32[1,32,2048]{2,1,0:T(8,128)} %mom_hbm.1) | copy-start | bytes 786436

commit v3 on v2

--- a/solution.py
+++ b/solution.py
@@ -36,9 +36,9 @@
 
 
 def kernel(
-    module_ref, owner_ref, x_hbm, outer_hbm, mom_hbm,
+    module_hbm, owner_hbm, x_hbm, outer_hbm, mom_hbm,
     new_outer_ref, new_mom_ref, fresh_ref,
-    x_v, outer_v, mom_v, x_send, x_recv, outer_recv, mom_recv, mean_send, mean_slab,
+    module_ref, owner_ref, x_v, outer_v, mom_v, x_send, x_recv, outer_recv, mom_recv, mean_send, mean_slab,
     fresh_send, fresh_recv, dp_recv, vec_recv, weights, select,
     load_sem, send_sem, recv_sem,
 ):
@@ -46,8 +46,11 @@
     plane = lax.axis_index("dp")
 
     loads = [
-        pltpu.make_async_copy(src.at[...], dst.at[...], load_sem.at[i])
-        for i, (src, dst) in enumerate(((x_hbm, x_v), (outer_hbm, outer_v), (mom_hbm, mom_v)))
+        pltpu.make_async_copy(src, dst, load_sem.at[i])
+        for i, (src, dst) in enumerate((
+            (x_hbm, x_v), (outer_hbm, outer_v), (mom_hbm, mom_v),
+            (module_hbm, module_ref), (owner_hbm, owner_ref),
+        ))
     ]
     for load in loads:
         load.start()
@@ -74,8 +77,8 @@
             for column in range(16):
                 chunk = (2 * half + part) * 16 + column
                 x_send[16 * chunk : 16 * chunk + 16, :] = both[:, 128 * column : 128 * column + 128]
-    loads[1].wait()
-    loads[2].wait()
+    for load in loads[1:]:
+        load.wait()
 
     pl.semaphore_wait(barrier, N - 1 + DP - 1)
 
@@ -203,19 +206,33 @@
     wait(send_sem.at[6], fresh_send, 16 * (N - 1))
 
 
+def write_out(a_ref, b_ref, c_ref, a_hbm, b_hbm, c_hbm, sem):
+    copies = [
+        pltpu.make_async_copy(src, dst, sem.at[i])
+        for i, (src, dst) in enumerate(((a_ref, a_hbm), (b_ref, b_hbm), (c_ref, c_hbm)))
+    ]
+    for copy in copies:
+        copy.start()
+    for copy in copies:
+        copy.wait()
+
+
 def local(path_params, path_module, owner_of, outer_params, momentum):
     vmem = pl.BlockSpec(memory_space=pltpu.VMEM)
-    anywhere = pl.BlockSpec(memory_space=pl.ANY)
-    return pl.pallas_call(
+    hbm = pl.BlockSpec(memory_space=pl.ANY)
+    shapes = (
+        jax.ShapeDtypeStruct((1, R, 2048), F32),
+        jax.ShapeDtypeStruct((1, R, 2048), F32),
+        jax.ShapeDtypeStruct((2, R, 2048), BF16),
+    )
+    results = pl.pallas_call(
         kernel,
-        out_shape=(
-            jax.ShapeDtypeStruct((1, R, 2048), F32),
-            jax.ShapeDtypeStruct((1, R, 2048), F32),
-            jax.ShapeDtypeStruct((2, R, 2048), BF16),
-        ),
-        in_specs=[vmem, pl.BlockSpec(memory_space=pltpu.SMEM), anywhere, anywhere, anywhere],
+        out_shape=shapes,
+        in_specs=[hbm] * 5,
         out_specs=(vmem, vmem, vmem),
         scratch_shapes=[
+            pltpu.VMEM((1, 128), jnp.int32),
+            pltpu.SMEM((MODULES,), jnp.int32),
             pltpu.VMEM((2, R, 2048), BF16),
             pltpu.VMEM((1, R, 2048), F32),
             pltpu.VMEM((1, R, 2048), F32),
@@ -231,14 +248,22 @@
             pltpu.VMEM((N, 128), F32),
             pltpu.VMEM((8 * N, 1024), BF16),
             pltpu.VMEM((1024, 8 * N), BF16),
-            pltpu.SemaphoreType.DMA((3,)),
+            pltpu.SemaphoreType.DMA((5,)),
             pltpu.SemaphoreType.DMA((7,)),
             pltpu.SemaphoreType.DMA((7,)),
         ],
         compiler_params=pltpu.CompilerParams(
-            collective_id=0, has_side_effects=True, vmem_limit_bytes=48 << 20
+            collective_id=0, has_side_effects=True, vmem_limit_bytes=53 << 20
         ),
     )(path_module.reshape(1, 128), owner_of, path_params, outer_params, momentum)
+    return pl.pallas_call(
+        write_out,
+        out_shape=shapes,
+        in_specs=[hbm] * 3,
+        out_specs=(hbm,) * 3,
+        scratch_shapes=[pltpu.SemaphoreType.DMA((3,))],
+        compiler_params=pltpu.CompilerParams(vmem_limit_bytes=1 << 20),
+    )(*results)
 
 
 def solution(mesh):

time: 55.8 us -> 51 us (0.914)
  local copies, waits for them, and re-layouts: 5.61 us -> 0.66 us
    unnamed x13 -> x4, local copies, waits for them, and re-layouts: 5.61 us -> 0.66 us
    pallas_call x1 -> x2, Pallas kernels: 49.4 us -> 49.6 us  [the longest x1 48.7 us: local(): pl.pallas_call(kernel, out_shape=shapes, in_specs=[hbm] * 5, out_specs=(v...]
where the time goes in v3:
time: 51 us; the launch traced here: 50.9 us
  Pallas kernels  49.6 us (97%)
  local copies, waits for them, and re-layouts  0.66 us (1%)
  between operations  0.66 us (1%)
    pallas_call x1, Pallas kernels, local(): pl.pallas_call(kernel, out_shape=shapes, in_specs=[hbm] * 5, out_specs=(v...  48.7 us

profile of v3, /device:TPU:1, one launch (start us, length us, event | category | flops | bytes accessed | tf_op | source)
XLA Modules:
  0.0 50.9 jit_solution(450184177951388233)
XLA Ops:
  0.6 0.0 copy-start.1
  0.6 0.0 copy-start
  0.7 0.6 %copy-done.1 = s32[16]{0:T(128)S(1)} copy-done((s32[16]{0:T(128)S(1)}, s32[16]{0:T(128)}, u32[]{:S(2)}) %copy-start.1) | copy-done | bytes 88
  1.3 0.0 copy-done
  1.3 48.7 %shard_map.76 = (f32[1,32,2048]{2,1,0:T(8,128)S(1)}, f32[1,32,2048]{2,1,0:T(8,128)S(1)}, bf16[2,32,2048]{2,1,0:T(8,128)(2,1)S(1)}) custom-call(s32[1,128]{1,0:T(1,128)S(1)} %bitcast.1, s32[16]{0:T(128)S(1)} %copy-done.1, bf16[2,32,2048]{2,1,0:T(8,128)(2,1)} %x_hbm.1, f32[1,32,2048]{2,1,0:T(8,128)} %outer_hbm.1, f32[1,32,2048]{2,1,0:T(8,128)} %mom_hbm.1), custom_call_target="tpu_custom_call" | custom-call | tf_op jit(solution)/shard_map/pallas_call | solution.py:228
  50.0 0.9 %shard_map.77 = (f32[1,32,2048]{2,1,0:T(8,128)}, f32[1,32,2048]{2,1,0:T(8,128)}, bf16[2,32,2048]{2,1,0:T(8,128)(2,1)}) custom-call(f32[1,32,2048]{2,1,0:T(8,128)S(1)} %get-tuple-element.6.a_ref, f32[1,32,2048]{2,1,0:T(8,128)S(1)} %get-tuple-element.7.b_ref, bf16[2,32,2048]{2,1,0:T(8,128)(2,1)S(1)} %get-tuple-element.8.c_ref), custom_call_target="tpu_custom_call" | custom-call | tf_op jit(solution)/shard_map/pallas_call | solution.py:259
Async XLA Ops:
  0.6 0.7 %copy-start.1 = (s32[16]{0:T(128)S(1)}, s32[16]{0:T(128)}, u32[]{:S(2)}) copy-start(s32[16]{0:T(128)} %owner_hbm.1) | copy-start | bytes 196
  0.6 0.7 %copy-start = (s32[128]{0:T(128)S(1)}, s32[128]{0:T(128)}, u32[]{:S(2)}) copy-start(s32[128]{0:T(128)} %param.6) | copy-start | bytes 1540

commit v4 on v3

--- a/solution.py
+++ b/solution.py
@@ -91,6 +91,25 @@
                 recv_sem=recv_sem.at[stage], device_id={"path": to}, device_id_type=MESH,
             ).start()
 
+    def send_early(stage, source, target):
+        @pl.loop(0, N)
+        def _(k):
+            i = lax.rem(k, 8)
+            y, core = lax.div(me, 16), lax.rem(me, 2)
+            z = lax.div(k, 8)
+            to = (
+                lax.rem(y + zig(lax.div(i, 2), 2), 4) * 16
+                + z * 2
+                + lax.rem(core + 1 - lax.rem(i, 2), 2)
+            )
+
+            @pl.when(to != me)
+            def _():
+                pltpu.make_async_remote_copy(
+                    src_ref=source(to), dst_ref=target, send_sem=send_sem.at[stage],
+                    recv_sem=recv_sem.at[stage], device_id={"path": to}, device_id_type=MESH,
+                ).start()
+
     def wait(sem, ref, count):
         view = ref.at[pl.ds(0, count)]
         pltpu.make_async_copy(view, view, sem).wait()
@@ -149,13 +168,13 @@
             send_sem=send_sem.at[3], recv_sem=recv_sem.at[3],
             device_id={"dp": lax.rem(plane + k, DP)}, device_id_type=MESH,
         ).start()
+    wait(recv_sem.at[3], dp_recv, DP - 1)
+    everywhere = dp_recv[0:1] + dp_recv[1:2] + dp_recv[2:3] + dp_recv[3:4]
+
+    vec_recv[pl.ds(me, 1), :] = everywhere
+    send_all(5, lambda to: vec_recv.at[pl.ds(me, 1)], vec_recv.at[pl.ds(me, 1)])
     send_all(4, lambda to: mean_send.at[rows(to, 8)], mean_slab.at[tile(me)])
     mean_slab[tile(me)[0], tile(me)[1]] = mean_send[rows(me, 8), :]
-    wait(recv_sem.at[3], dp_recv, DP - 1)
-    everywhere = dp_recv[0:1] + dp_recv[1:2] + dp_recv[2:3] + dp_recv[3:4]
-
-    vec_recv[pl.ds(me, 1), :] = everywhere
-    send_all(5, lambda to: vec_recv.at[pl.ds(me, 1)], vec_recv.at[pl.ds(me, 1)])
     wait(recv_sem.at[2], mom_recv, 8 * (N - 1))
     limit = 0.5 * (float(R * FF) ** 0.5)
     wait(recv_sem.at[5], vec_recv, N - 1)
@@ -169,7 +188,7 @@
     fresh_send[...] = jnp.dot(
         select[...], theta.astype(BF16), preferred_element_type=F32
     ).astype(BF16)
-    send_all(6, lambda to: fresh_send.at[rows(to, 16)], fresh_recv.at[rows(me, 16)])
+    send_early(6, lambda to: fresh_send.at[rows(to, 16)], fresh_recv.at[rows(me, 16)])
     fresh_recv[rows(me, 16), :] = fresh_send[rows(me, 16), :]
 
     held_slot = held_here > 0

time: 51 us -> 47.8 us (0.937)
  Pallas kernels: 49.6 us -> 45.9 us
    pallas_call x1, Pallas kernels: 48.7 us -> 45 us  [local(): pl.pallas_call(kernel, out_shape=shapes, in_specs=[hbm] * 5, out_specs=(v...]
where the time goes in v4:
time: 47.8 us; the launch traced here: 47.2 us
  Pallas kernels  45.9 us (96%)
  local copies, waits for them, and re-layouts  0.66 us (1%)
  between operations  0.66 us (1%)
    pallas_call x1, Pallas kernels, local(): pl.pallas_call(kernel, out_shape=shapes, in_specs=[hbm] * 5, out_specs=(v...  45 us

profile of v4, /device:TPU:1, one launch (start us, length us, event | category | flops | bytes accessed | tf_op | source)
XLA Modules:
  0.0 47.2 jit_solution(12037753327278357685)
XLA Ops:
  0.6 0.0 copy-start.1
  0.6 0.0 copy-start
  0.7 0.6 %copy-done.1 = s32[16]{0:T(128)S(1)} copy-done((s32[16]{0:T(128)S(1)}, s32[16]{0:T(128)}, u32[]{:S(2)}) %copy-start.1) | copy-done | bytes 88
  1.3 0.0 copy-done
  1.3 45.0 %shard_map.76 = (f32[1,32,2048]{2,1,0:T(8,128)S(1)}, f32[1,32,2048]{2,1,0:T(8,128)S(1)}, bf16[2,32,2048]{2,1,0:T(8,128)(2,1)S(1)}) custom-call(s32[1,128]{1,0:T(1,128)S(1)} %bitcast.1, s32[16]{0:T(128)S(1)} %copy-done.1, bf16[2,32,2048]{2,1,0:T(8,128)(2,1)} %x_hbm.1, f32[1,32,2048]{2,1,0:T(8,128)} %outer_hbm.1, f32[1,32,2048]{2,1,0:T(8,128)} %mom_hbm.1), custom_call_target="tpu_custom_call" | custom-call | tf_op jit(solution)/shard_map/pallas_call | solution.py:247
  46.3 0.9 %shard_map.77 = (f32[1,32,2048]{2,1,0:T(8,128)}, f32[1,32,2048]{2,1,0:T(8,128)}, bf16[2,32,2048]{2,1,0:T(8,128)(2,1)}) custom-call(f32[1,32,2048]{2,1,0:T(8,128)S(1)} %get-tuple-element.6.a_ref, f32[1,32,2048]{2,1,0:T(8,128)S(1)} %get-tuple-element.7.b_ref, bf16[2,32,2048]{2,1,0:T(8,128)(2,1)S(1)} %get-tuple-element.8.c_ref), custom_call_target="tpu_custom_call" | custom-call | tf_op jit(solution)/shard_map/pallas_call | solution.py:278
Async XLA Ops:
  0.6 0.7 %copy-start.1 = (s32[16]{0:T(128)S(1)}, s32[16]{0:T(128)}, u32[]{:S(2)}) copy-start(s32[16]{0:T(128)} %owner_hbm.1) | copy-start | bytes 196
  0.6 0.7 %copy-start = (s32[128]{0:T(128)S(1)}, s32[128]{0:T(128)}, u32[]{:S(2)}) copy-start(s32[128]{0:T(128)} %param.6) | copy-start | bytes 1540

commit v5 on v4

--- a/solution.py
+++ b/solution.py
@@ -57,7 +57,7 @@
 
     barrier = pltpu.get_barrier_semaphore()
 
-    @pl.loop(0, N - 1)
+    @pl.loop(0, N - 1, unroll=3)
     def _(k):
         pl.semaphore_signal(barrier, inc=1, device_id={"path": peer(me, k)}, device_id_type=MESH)
 
@@ -83,7 +83,7 @@
     pl.semaphore_wait(barrier, N - 1 + DP - 1)
 
     def send_all(stage, source, target):
-        @pl.loop(0, N - 1)
+        @pl.loop(0, N - 1, unroll=3)
         def _(k):
             to = peer(me, k)
             pltpu.make_async_remote_copy(
@@ -92,16 +92,11 @@
             ).start()
 
     def send_early(stage, source, target):
-        @pl.loop(0, N)
+        @pl.loop(0, N, unroll=2)
         def _(k):
-            i = lax.rem(k, 8)
-            y, core = lax.div(me, 16), lax.rem(me, 2)
-            z = lax.div(k, 8)
-            to = (
-                lax.rem(y + zig(lax.div(i, 2), 2), 4) * 16
-                + z * 2
-                + lax.rem(core + 1 - lax.rem(i, 2), 2)
-            )
+            y, z, core = lax.div(me, 16), lax.rem(lax.div(me, 2), 8), lax.rem(me, 2)
+            dy, dz, dc = lax.rem(lax.div(k, 8), 4), lax.rem(lax.div(k, 2), 4), lax.rem(k, 2)
+            to = dy * 16 + (lax.div(k, 32) * 4 + lax.rem(z + dz, 4)) * 2 + lax.rem(core + dc, 2)
 
             @pl.when(to != me)
             def _():

time: 47.8 us -> 46.9 us (0.981)
  Pallas kernels: 45.9 us -> 45.1 us
    pallas_call x1, Pallas kernels: 45 us -> 44.2 us  [local(): pl.pallas_call(kernel, out_shape=shapes, in_specs=[hbm] * 5, out_specs=(v...]
where the time goes in v5:
time: 46.9 us; the launch traced here: 46.4 us
  Pallas kernels  45.1 us (96%)
  local copies, waits for them, and re-layouts  0.66 us (1%)
  between operations  0.66 us (1%)
    pallas_call x1, Pallas kernels, local(): pl.pallas_call(kernel, out_shape=shapes, in_specs=[hbm] * 5, out_specs=(v...  44.2 us

profile of v5, /device:TPU:1, one launch (start us, length us, event | category | flops | bytes accessed | tf_op | source)
XLA Modules:
  0.0 46.4 jit_solution(17694795022424455321)
XLA Ops:
  0.6 0.0 copy-start.1
  0.6 0.0 copy-start
  0.7 0.6 %copy-done.1 = s32[16]{0:T(128)S(1)} copy-done((s32[16]{0:T(128)S(1)}, s32[16]{0:T(128)}, u32[]{:S(2)}) %copy-start.1) | copy-done | bytes 88
  1.3 0.0 copy-done
  1.3 44.2 %shard_map.76 = (f32[1,32,2048]{2,1,0:T(8,128)S(1)}, f32[1,32,2048]{2,1,0:T(8,128)S(1)}, bf16[2,32,2048]{2,1,0:T(8,128)(2,1)S(1)}) custom-call(s32[1,128]{1,0:T(1,128)S(1)} %bitcast.1, s32[16]{0:T(128)S(1)} %copy-done.1, bf16[2,32,2048]{2,1,0:T(8,128)(2,1)} %x_hbm.1, f32[1,32,2048]{2,1,0:T(8,128)} %outer_hbm.1, f32[1,32,2048]{2,1,0:T(8,128)} %mom_hbm.1), custom_call_target="tpu_custom_call" | custom-call | tf_op jit(solution)/shard_map/pallas_call | solution.py:242
  45.5 0.9 %shard_map.77 = (f32[1,32,2048]{2,1,0:T(8,128)}, f32[1,32,2048]{2,1,0:T(8,128)}, bf16[2,32,2048]{2,1,0:T(8,128)(2,1)}) custom-call(f32[1,32,2048]{2,1,0:T(8,128)S(1)} %get-tuple-element.6.a_ref, f32[1,32,2048]{2,1,0:T(8,128)S(1)} %get-tuple-element.7.b_ref, bf16[2,32,2048]{2,1,0:T(8,128)(2,1)S(1)} %get-tuple-element.8.c_ref), custom_call_target="tpu_custom_call" | custom-call | tf_op jit(solution)/shard_map/pallas_call | solution.py:273
Async XLA Ops:
  0.6 0.7 %copy-start.1 = (s32[16]{0:T(128)S(1)}, s32[16]{0:T(128)}, u32[]{:S(2)}) copy-start(s32[16]{0:T(128)} %owner_hbm.1) | copy-start | bytes 196
  0.6 0.7 %copy-start = (s32[128]{0:T(128)S(1)}, s32[128]{0:T(128)}, u32[]{:S(2)}) copy-start(s32[128]{0:T(128)} %param.6) | copy-start | bytes 1540

commit v6 on v5

--- a/solution.py
+++ b/solution.py
@@ -11,6 +11,7 @@
 N = 64
 DP = 4
 MESH = pl.DeviceIdType.MESH
+LINE = ((2, 1), (2, 0), (1, 1), (1, 0), (3, 1), (3, 0), (0, 1))
 F32 = jnp.float32
 BF16 = jnp.bfloat16
 
@@ -40,7 +41,7 @@
     new_outer_ref, new_mom_ref, fresh_ref,
     module_ref, owner_ref, x_v, outer_v, mom_v, x_send, x_recv, outer_recv, mom_recv, mean_send, mean_slab,
     fresh_send, fresh_recv, dp_recv, vec_recv, weights, select,
-    load_sem, send_sem, recv_sem,
+    load_sem, send_sem, recv_sem, plane_sem,
 ):
     me = lax.axis_index("path")
     plane = lax.axis_index("dp")
@@ -57,14 +58,13 @@
 
     barrier = pltpu.get_barrier_semaphore()
 
-    @pl.loop(0, N - 1, unroll=3)
+    @pl.loop(0, N - 1, unroll=9)
     def _(k):
         pl.semaphore_signal(barrier, inc=1, device_id={"path": peer(me, k)}, device_id_type=MESH)
 
     for k in range(1, DP):
-        pl.semaphore_signal(
-            barrier, inc=1, device_id={"dp": lax.rem(plane + k, DP)}, device_id_type=MESH
-        )
+        to = {"dp": lax.rem(plane + k, DP)}
+        pl.semaphore_signal(barrier, inc=1, device_id=to, device_id_type=MESH)
 
     loads[0].wait()
     for half in range(2):
@@ -83,7 +83,7 @@
     pl.semaphore_wait(barrier, N - 1 + DP - 1)
 
     def send_all(stage, source, target):
-        @pl.loop(0, N - 1, unroll=3)
+        @pl.loop(0, N - 1, unroll=9)
         def _(k):
             to = peer(me, k)
             pltpu.make_async_remote_copy(
@@ -92,7 +92,7 @@
             ).start()
 
     def send_early(stage, source, target):
-        @pl.loop(0, N, unroll=2)
+        @pl.loop(0, N, unroll=8)
         def _(k):
             y, z, core = lax.div(me, 16), lax.rem(lax.div(me, 2), 8), lax.rem(me, 2)
             dy, dz, dc = lax.rem(lax.div(k, 8), 4), lax.rem(lax.div(k, 2), 4), lax.rem(k, 2)
@@ -112,6 +112,9 @@
     send_all(0, lambda to: x_send.at[rows(to, 16)], x_recv.at[rows(me, 16)])
     send_all(1, lambda to: outer_v.at[0].at[tile(to)], outer_recv.at[rows(me, 8)])
     send_all(2, lambda to: mom_v.at[0].at[tile(to)], mom_recv.at[rows(me, 8)])
+    for k in range(1, DP):
+        to = {"dp": lax.rem(plane + k, DP)}
+        pl.semaphore_signal(plane_sem, inc=1, device_id=to, device_id_type=MESH)
     x_recv[rows(me, 16), :] = x_send[rows(me, 16), :]
     outer_recv[rows(me, 8), :] = outer_v[0, tile(me)[0], tile(me)[1]]
     mom_recv[rows(me, 8), :] = mom_v[0, tile(me)[0], tile(me)[1]]
@@ -156,23 +159,41 @@
     squares = jnp.sum(pseudo * pseudo, axis=1, keepdims=True)
     squares = jnp.sum(jnp.where(diagonal, squares, 0.0), axis=0, keepdims=True)
 
-    dp_recv[pl.ds(plane, 1), :] = squares
-    for k in range(1, DP):
-        pltpu.make_async_remote_copy(
-            src_ref=dp_recv.at[pl.ds(plane, 1)], dst_ref=dp_recv.at[pl.ds(plane, 1)],
-            send_sem=send_sem.at[3], recv_sem=recv_sem.at[3],
-            device_id={"dp": lax.rem(plane + k, DP)}, device_id_type=MESH,
-        ).start()
-    wait(recv_sem.at[3], dp_recv, DP - 1)
-    everywhere = dp_recv[0:1] + dp_recv[1:2] + dp_recv[2:3] + dp_recv[3:4]
-
-    vec_recv[pl.ds(me, 1), :] = everywhere
-    send_all(5, lambda to: vec_recv.at[pl.ds(me, 1)], vec_recv.at[pl.ds(me, 1)])
+    core = lax.rem(me, 2)
+    dp_recv[pl.ds(core, 1), :] = squares
+    pltpu.make_async_remote_copy(
+        src_ref=dp_recv.at[pl.ds(core, 1)], dst_ref=dp_recv.at[pl.ds(core, 1)],
+        send_sem=send_sem.at[3], recv_sem=recv_sem.at[3],
+        device_id={"path": me + 1 - 2 * core}, device_id_type=MESH,
+    ).start()
+    pl.semaphore_wait(plane_sem, DP - 1)
+    wait(recv_sem.at[3], dp_recv, 1)
+    chip = pl.ds(plane * (N // 2) + lax.div(me, 2), 1)
+    vec_recv[chip, :] = dp_recv[0:1] + dp_recv[1:2]
+
+    def to_chips(count, unroll, plane_of):
+        @pl.loop(0, count, unroll=unroll)
+        def _(k):
+            y, z = lax.div(me, 16), lax.rem(lax.div(me, 2), 8)
+            to = (
+                lax.rem(y + zig(lax.rem(lax.div(k, 8), 4), 2), 4) * 16
+                + lax.rem(z + zig(lax.rem(k, 8), 4), 8) * 2
+                + core
+            )
+            pltpu.make_async_remote_copy(
+                src_ref=vec_recv.at[chip], dst_ref=vec_recv.at[chip],
+                send_sem=send_sem.at[5], recv_sem=recv_sem.at[5],
+                device_id={"path": to, "dp": plane_of(k)}, device_id_type=MESH,
+            ).start()
+
+    to_chips(3 * N // 2, 4, lambda k: lax.rem(plane + zig(lax.div(k, 32), 2), DP))
+    to_chips(N // 2 - 1, 1, lambda k: plane)
+
     send_all(4, lambda to: mean_send.at[rows(to, 8)], mean_slab.at[tile(me)])
     mean_slab[tile(me)[0], tile(me)[1]] = mean_send[rows(me, 8), :]
     wait(recv_sem.at[2], mom_recv, 8 * (N - 1))
     limit = 0.5 * (float(R * FF) ** 0.5)
-    wait(recv_sem.at[5], vec_recv, N - 1)
+    wait(recv_sem.at[5], vec_recv, 2 * N - 1)
     total = jnp.sum(vec_recv[...], axis=0, keepdims=True)
     factors = jnp.minimum(1.0, limit / jnp.sqrt(total + 1e-06))
 
@@ -214,9 +235,9 @@
     wait(send_sem.at[0], x_send, 16 * (N - 1))
     wait(send_sem.at[1], outer_recv, 8 * (N - 1))
     wait(send_sem.at[2], mom_recv, 8 * (N - 1))
-    wait(send_sem.at[3], dp_recv, DP - 1)
+    wait(send_sem.at[3], dp_recv, 1)
     wait(send_sem.at[4], mean_send, 8 * (N - 1))
-    wait(send_sem.at[5], vec_recv, N - 1)
+    wait(send_sem.at[5], vec_recv, 2 * N - 1)
     wait(send_sem.at[6], fresh_send, 16 * (N - 1))
 
 
@@ -258,13 +279,14 @@
             pltpu.VMEM((R, 2048), F32),
             pltpu.VMEM((16 * N, 128), BF16),
             pltpu.VMEM((16 * N, 128), BF16),
-            pltpu.VMEM((DP, 128), F32),
-            pltpu.VMEM((N, 128), F32),
+            pltpu.VMEM((2, 128), F32),
+            pltpu.VMEM((2 * N, 128), F32),
             pltpu.VMEM((8 * N, 1024), BF16),
             pltpu.VMEM((1024, 8 * N), BF16),
             pltpu.SemaphoreType.DMA((5,)),
             pltpu.SemaphoreType.DMA((7,)),
             pltpu.SemaphoreType.DMA((7,)),
+            pltpu.SemaphoreType.REGULAR,
         ],
         compiler_params=pltpu.CompilerParams(
             collective_id=0, has_side_effects=True, vmem_limit_bytes=53 << 20

time: 46.9 us -> 46 us (0.981)
  Pallas kernels: 45.1 us -> 44.5 us
    pallas_call x1, Pallas kernels: 44.2 us -> 43.6 us  [local(): pl.pallas_call(kernel, out_shape=shapes, in_specs=[hbm] * 5, out_specs=(v...]
where the time goes in v6:
time: 46 us; the launch traced here: 45.8 us
  Pallas kernels  44.5 us (97%)
  local copies, waits for them, and re-layouts  0.66 us (1%)
  between operations  0.66 us (1%)
    pallas_call x1, Pallas kernels, local(): pl.pallas_call(kernel, out_shape=shapes, in_specs=[hbm] * 5, out_specs=(v...  43.6 us

profile of v6, /device:TPU:1, one launch (start us, length us, event | category | flops | bytes accessed | tf_op | source)
XLA Modules:
  0.0 45.8 jit_solution(2577392975738208367)
XLA Ops:
  0.6 0.0 copy-start.1
  0.6 0.0 copy-start
  0.7 0.6 %copy-done.1 = s32[16]{0:T(128)S(1)} copy-done((s32[16]{0:T(128)S(1)}, s32[16]{0:T(128)}, u32[]{:S(2)}) %copy-start.1) | copy-done | bytes 88
  1.3 0.0 copy-done
  1.3 43.6 %shard_map.76 = (f32[1,32,2048]{2,1,0:T(8,128)S(1)}, f32[1,32,2048]{2,1,0:T(8,128)S(1)}, bf16[2,32,2048]{2,1,0:T(8,128)(2,1)S(1)}) custom-call(s32[1,128]{1,0:T(1,128)S(1)} %bitcast.1, s32[16]{0:T(128)S(1)} %copy-done.1, bf16[2,32,2048]{2,1,0:T(8,128)(2,1)} %x_hbm.1, f32[1,32,2048]{2,1,0:T(8,128)} %outer_hbm.1, f32[1,32,2048]{2,1,0:T(8,128)} %mom_hbm.1), custom_call_target="tpu_custom_call" | custom-call | tf_op jit(solution)/shard_map/pallas_call | solution.py:263
  44.9 0.9 %shard_map.77 = (f32[1,32,2048]{2,1,0:T(8,128)}, f32[1,32,2048]{2,1,0:T(8,128)}, bf16[2,32,2048]{2,1,0:T(8,128)(2,1)}) custom-call(f32[1,32,2048]{2,1,0:T(8,128)S(1)} %get-tuple-element.6.a_ref, f32[1,32,2048]{2,1,0:T(8,128)S(1)} %get-tuple-element.7.b_ref, bf16[2,32,2048]{2,1,0:T(8,128)(2,1)S(1)} %get-tuple-element.8.c_ref), custom_call_target="tpu_custom_call" | custom-call | tf_op jit(solution)/shard_map/pallas_call | solution.py:295
Async XLA Ops:
  0.6 0.7 %copy-start.1 = (s32[16]{0:T(128)S(1)}, s32[16]{0:T(128)}, u32[]{:S(2)}) copy-start(s32[16]{0:T(128)} %owner_hbm.1) | copy-start | bytes 196
  0.6 0.7 %copy-start = (s32[128]{0:T(128)S(1)}, s32[128]{0:T(128)}, u32[]{:S(2)}) copy-start(s32[128]{0:T(128)} %param.6) | copy-start | bytes 1540

commit v7 on v6

--- a/solution.py
+++ b/solution.py
@@ -58,7 +58,7 @@
 
     barrier = pltpu.get_barrier_semaphore()
 
-    @pl.loop(0, N - 1, unroll=9)
+    @pl.loop(0, N - 1, unroll=21)
     def _(k):
         pl.semaphore_signal(barrier, inc=1, device_id={"path": peer(me, k)}, device_id_type=MESH)
 
@@ -83,7 +83,7 @@
     pl.semaphore_wait(barrier, N - 1 + DP - 1)
 
     def send_all(stage, source, target):
-        @pl.loop(0, N - 1, unroll=9)
+        @pl.loop(0, N - 1, unroll=21)
         def _(k):
             to = peer(me, k)
             pltpu.make_async_remote_copy(
@@ -91,8 +91,8 @@
                 recv_sem=recv_sem.at[stage], device_id={"path": to}, device_id_type=MESH,
             ).start()
 
-    def send_early(stage, source, target):
-        @pl.loop(0, N, unroll=8)
+    def send_early(stage, source, target, first=0, last=N):
+        @pl.loop(first, last, unroll=8)
         def _(k):
             y, z, core = lax.div(me, 16), lax.rem(lax.div(me, 2), 8), lax.rem(me, 2)
             dy, dz, dc = lax.rem(lax.div(k, 8), 4), lax.rem(lax.div(k, 2), 4), lax.rem(k, 2)
@@ -186,10 +186,10 @@
                 device_id={"path": to, "dp": plane_of(k)}, device_id_type=MESH,
             ).start()
 
-    to_chips(3 * N // 2, 4, lambda k: lax.rem(plane + zig(lax.div(k, 32), 2), DP))
-    to_chips(N // 2 - 1, 1, lambda k: plane)
-
-    send_all(4, lambda to: mean_send.at[rows(to, 8)], mean_slab.at[tile(me)])
+    to_chips(3 * N // 2, 32, lambda k: lax.rem(plane + zig(lax.div(k, 32), 2), DP))
+    to_chips(N // 2 - 1, 31, lambda k: plane)
+
+    send_early(4, lambda to: mean_send.at[rows(to, 8)], mean_slab.at[tile(me)], 0, N)
     mean_slab[tile(me)[0], tile(me)[1]] = mean_send[rows(me, 8), :]
     wait(recv_sem.at[2], mom_recv, 8 * (N - 1))
     limit = 0.5 * (float(R * FF) ** 0.5)

time: 46 us -> 45.3 us (0.985)
  Pallas kernels: 44.5 us -> 43.7 us
    pallas_call x1, Pallas kernels: 43.6 us -> 42.8 us  [local(): pl.pallas_call(kernel, out_shape=shapes, in_specs=[hbm] * 5, out_specs=(v...]
where the time goes in v7:
time: 45.3 us; the launch traced here: 45 us
  Pallas kernels  43.7 us (96%)
  local copies, waits for them, and re-layouts  0.66 us (1%)
  between operations  0.66 us (1%)
    pallas_call x1, Pallas kernels, local(): pl.pallas_call(kernel, out_shape=shapes, in_specs=[hbm] * 5, out_specs=(v...  42.8 us

profile of v7, /device:TPU:1, one launch (start us, length us, event | category | flops | bytes accessed | tf_op | source)
XLA Modules:
  0.0 45.0 jit_solution(7465563443598252500)
XLA Ops:
  0.6 0.0 copy-start.1
  0.6 0.0 copy-start
  0.7 0.6 %copy-done.1 = s32[16]{0:T(128)S(1)} copy-done((s32[16]{0:T(128)S(1)}, s32[16]{0:T(128)}, u32[]{:S(2)}) %copy-start.1) | copy-done | bytes 88
  1.3 0.0 copy-done
  1.3 42.8 %shard_map.76 = (f32[1,32,2048]{2,1,0:T(8,128)S(1)}, f32[1,32,2048]{2,1,0:T(8,128)S(1)}, bf16[2,32,2048]{2,1,0:T(8,128)(2,1)S(1)}) custom-call(s32[1,128]{1,0:T(1,128)S(1)} %bitcast.1, s32[16]{0:T(128)S(1)} %copy-done.1, bf16[2,32,2048]{2,1,0:T(8,128)(2,1)} %x_hbm.1, f32[1,32,2048]{2,1,0:T(8,128)} %outer_hbm.1, f32[1,32,2048]{2,1,0:T(8,128)} %mom_hbm.1), custom_call_target="tpu_custom_call" | custom-call | tf_op jit(solution)/shard_map/pallas_call | solution.py:263
  44.1 0.9 %shard_map.77 = (f32[1,32,2048]{2,1,0:T(8,128)}, f32[1,32,2048]{2,1,0:T(8,128)}, bf16[2,32,2048]{2,1,0:T(8,128)(2,1)}) custom-call(f32[1,32,2048]{2,1,0:T(8,128)S(1)} %get-tuple-element.6.a_ref, f32[1,32,2048]{2,1,0:T(8,128)S(1)} %get-tuple-element.7.b_ref, bf16[2,32,2048]{2,1,0:T(8,128)(2,1)S(1)} %get-tuple-element.8.c_ref), custom_call_target="tpu_custom_call" | custom-call | tf_op jit(solution)/shard_map/pallas_call | solution.py:295
Async XLA Ops:
  0.6 0.7 %copy-start.1 = (s32[16]{0:T(128)S(1)}, s32[16]{0:T(128)}, u32[]{:S(2)}) copy-start(s32[16]{0:T(128)} %owner_hbm.1) | copy-start | bytes 196
  0.6 0.7 %copy-start = (s32[128]{0:T(128)S(1)}, s32[128]{0:T(128)}, u32[]{:S(2)}) copy-start(s32[128]{0:T(128)} %param.6) | copy-start | bytes 1540
